TPU v7x, 32 devices: a whole 2x2x4 slice. The times are simulated.
32 devices in a mesh: dom: 2 (over x), hst: 16 (over z, y, core).
Axes of the slice: x: 2, y: 2, z: 4, core: 2. Of those that a mesh axis runs over, the one named last changes fastest.
Arguments:
- queries: bfloat16 [8192, 4096], P(('dom', 'hst')), parts along dimension 0, may hold values from -96 to 96
- suf_keys: bfloat16 [8192, 512], P(('dom', 'hst')), parts along dimension 0, may hold values from -4 to 4
- suf_values: bfloat16 [8192, 512], P(('dom', 'hst')), parts along dimension 0, may hold values from -30 to 30
- cache_keys: bfloat16 [1024, 16, 512], P(('dom', 'hst')), parts along dimension 0, may hold values from -6 to 6
- cache_values: bfloat16 [1024, 16, 512], P(('dom', 'hst')), parts along dimension 0, may hold values from -30 to 30
- fetch_owner: int32 [32, 128], P(('dom', 'hst')), parts along dimension 0, may hold values from 0 to 15, as said below
- fetch_page: int32 [32, 128], P(('dom', 'hst')), parts along dimension 0, may hold values from 0 to 31
- prefix_len: int32 [32], P(('dom', 'hst')), parts along dimension 0, may hold values from 1 to 2048, as said below
Outputs:
- attended: bfloat16 [8192, 4096], P(('dom', 'hst')), parts along dimension 0
There are 2 independent parts, one for each index of `dom`. A program takes and returns all parts, laid end to end along the dimension named above; each array names one. Nothing has to cross between parts.
Inputs may be any that keep to these rules, and one draw needn't show every extreme that they name: `fetch_owner`: each request's row names every device exactly 8 times. `prefix_len`: in every draw at least one request has a prefix of exactly 2048 tokens, filling all its page slots.
All inputs are finite; a program needn't handle non-finite values.
Results may differ from a plain program's by a relative error of at most 0.0055.
Values may be sent and summed in bfloat16 or wider, within the bound.
A program may use at most 64 MiB of HBM per device.

v0:
```python
import jax
import jax.numpy as jnp
from jax import lax
from jax.sharding import PartitionSpec as P

HD = 128


MASKED = -1e30


def partial_terms(query_rows, key_rows, value_rows, visible, score_scale):
    scores = (
        lax.dot_general(
            query_rows, key_rows, (((1,), (1,)), ((), ())), preferred_element_type=jnp.float32
        )
        * score_scale
    )
    scores = jnp.where(visible, scores, MASKED)
    row_max = jnp.max(scores, axis=1)
    weights = jnp.where(visible, jnp.exp(scores - row_max[:, None]), jnp.float32(0.0))
    weight_sum = jnp.sum(weights, axis=1)
    summed = jnp.dot(weights.astype(jnp.bfloat16), value_rows, preferred_element_type=jnp.float32)
    return (row_max, weight_sum, summed)


def blocked_terms(query_rows, row_token, key_rows, value_rows, visible_for, score_scale):
    row_count = query_rows.shape[0]
    block_rows = min(512, row_count)
    block_count = row_count // block_rows
    row_blocks = query_rows.reshape(block_count, block_rows, query_rows.shape[1])
    token_blocks = row_token.reshape(block_count, block_rows)

    def one_block(block_pair):
        return partial_terms(
            block_pair[0], key_rows, value_rows, visible_for(block_pair[1]), score_scale
        )

    row_max, weight_sum, summed = lax.map(one_block, (row_blocks, token_blocks))
    return (
        row_max.reshape(row_count),
        weight_sum.reshape(row_count),
        summed.reshape(row_count, -1),
    )


def shards(
    queries, suf_keys, suf_values, cache_keys, cache_values, fetch_owner, fetch_page, prefix_len
):
    host_count = lax.axis_size("hst")
    own_index = lax.axis_index("hst")
    slot_count = fetch_owner.shape[1]
    capacity = slot_count // host_count
    page_rows = cache_keys.shape[1]
    kv_width = cache_keys.shape[2]
    suffix = queries.shape[0]
    kv_heads = kv_width // HD
    group_size = queries.shape[1] // kv_width
    score_scale = HD ** (-0.5)
    owners = fetch_owner[0]
    length = prefix_len[0]
    peer_ids = jnp.arange(host_count, dtype=jnp.int32)
    owner_hits = (owners[:, None] == peer_ids[None, :]).astype(jnp.int32)
    before = jnp.cumsum(owner_hits, axis=0) - owner_hits
    owner_rank = jnp.sum(before * owner_hits, axis=1)
    slot_of = owners * capacity + owner_rank
    slot_ids = jnp.arange(slot_count, dtype=jnp.int32)
    slot_match = (slot_of[None, :] == slot_ids[:, None]).astype(jnp.int32)
    position = jnp.sum(slot_match * slot_ids[None, :], axis=1)
    all_owners, all_pages = (
        lax.all_gather(fetch_owner, "hst", axis=0, tiled=True),
        lax.all_gather(fetch_page, "hst", axis=0, tiled=True),
    )
    from_me = (all_owners == own_index).astype(jnp.int32)
    send_rank = jnp.cumsum(from_me, axis=1) - from_me
    level_ids = jnp.arange(capacity, dtype=jnp.int32)
    picked = from_me[:, :, None] * (send_rank[:, :, None] == level_ids[None, None, :]).astype(
        jnp.int32
    )
    served = jnp.sum(picked * all_pages[:, :, None], axis=1)
    flat_served = served.reshape(-1)
    sent_keys = cache_keys[flat_served].reshape(host_count, capacity, page_rows, kv_width)
    sent_values = cache_values[flat_served].reshape(host_count, capacity, page_rows, kv_width)
    row_token = jnp.arange(suffix * group_size, dtype=jnp.int32) // group_size
    suffix_ids = jnp.arange(suffix, dtype=jnp.int32)
    page_offsets = jnp.arange(page_rows, dtype=jnp.int32)
    head_rows = [
        queries[:, kv_head * group_size * HD : (kv_head + 1) * group_size * HD].reshape(
            suffix * group_size, HD
        )
        for kv_head in range(kv_heads)
    ]

    def causal_for(block_tokens):
        return suffix_ids[None, :] <= block_tokens[:, None]

    got_keys, got_values = (
        lax.all_to_all(
            sent_keys.reshape(host_count, capacity * page_rows, kv_width),
            "hst",
            split_axis=0,
            concat_axis=0,
            tiled=True,
        ),
        lax.all_to_all(
            sent_values.reshape(host_count, capacity * page_rows, kv_width),
            "hst",
            split_axis=0,
            concat_axis=0,
            tiled=True,
        ),
    )
    key_rows = jnp.concatenate(
        [got_keys.reshape(slot_count * page_rows, kv_width), suf_keys], axis=0
    )
    value_rows = jnp.concatenate(
        [got_values.reshape(slot_count * page_rows, kv_width), suf_values], axis=0
    )
    prefix_ok = (position[:, None] * page_rows + page_offsets[None, :]).reshape(-1) < length

    def visible_for(block_tokens):
        prefix_part = jnp.broadcast_to(
            prefix_ok[None, :], (block_tokens.shape[0], prefix_ok.shape[0])
        )
        return jnp.concatenate([prefix_part, causal_for(block_tokens)], axis=1)

    states = [
        blocked_terms(
            head_rows[kv_head],
            row_token,
            key_rows[:, kv_head * HD : (kv_head + 1) * HD],
            value_rows[:, kv_head * HD : (kv_head + 1) * HD],
            visible_for,
            score_scale,
        )
        for kv_head in range(kv_heads)
    ]
    results = [(state[2] / state[1][:, None]).reshape(suffix, group_size * HD) for state in states]
    return jnp.concatenate(results, axis=1).astype(jnp.bfloat16)


def solution(mesh):
    in_specs = (
        P(("dom", "hst"), None),
        P(("dom", "hst"), None),
        P(("dom", "hst"), None),
        P(("dom", "hst"), None, None),
        P(("dom", "hst"), None, None),
        P(("dom", "hst"), None),
        P(("dom", "hst"), None),
        P(("dom", "hst")),
    )
    out_specs = P(("dom", "hst"), None)
    return jax.shard_map(shards, mesh=mesh, in_specs=in_specs, out_specs=out_specs, check_vma=False)
```

profile of v0, /device:TPU:13, one launch (start us, length us, event | category | flops | bytes accessed | tf_op | source)
XLA Modules:
  0.0 254.4 jit_solution(4016029419731390875)
XLA Ops:
  0.0 15.7 %all-gather = s32[16,1,128]{2,1,0:T(1,128)S(1)} all-gather(s32[1,1,128]{2,1,0:T(1,128)} %bitcast.160), channel_id=1, replica_groups=mesh['dom'=2,'hst'=16] {'hst'}, dimensions={0}, use_global_device_ids=true | all-gather | bytes 8704 | tf_op jit(solution)/shard_map/all_gather | solution.py:71
  16.0 21.4 %all-gather.1 = s32[16,1,128]{2,1,0:T(1,128)S(1)} all-gather(s32[1,1,128]{2,1,0:T(1,128)} %bitcast.163), channel_id=1, replica_groups=mesh['dom'=2,'hst'=16] {'hst'}, dimensions={0}, use_global_device_ids=true | all-gather | bytes 8704 | tf_op jit(solution)/shard_map/all_gather | solution.py:72
  39.9 6.6 %all-to-all-start = ((bf16[16,128,512]{2,1,0:T(8,128)(2,1)}), bf16[16,128,512]{2,1,0:T(8,128)(2,1)S(1)}, u32[]{:S(2)}, u32[]{:S(2)}) async-start(bf16[16,128,512]{2,1,0:T(8,128)(2,1)} %bitcast.144), calls=%async_computation | async-start | bytes 4194304 | tf_op jit(solution)/shard_map/all_to_all | solution.py:98
  48.4 45.5 %all-to-all-done = bf16[16,128,512]{2,1,0:T(8,128)(2,1)S(1)} async-done(((bf16[16,128,512]{2,1,0:T(8,128)(2,1)}), bf16[16,128,512]{2,1,0:T(8,128)(2,1)S(1)}, u32[]{:S(2)}, u32[]{:S(2)}) %all-to-all-start) | async-done | bytes 2097184 | tf_op jit(solution)/shard_map/all_to_all | solution.py:98
  93.9 4.9 %all-to-all-start.1 = ((bf16[16,128,512]{2,1,0:T(8,128)(2,1)}), bf16[16,128,512]{2,1,0:T(8,128)(2,1)}, u32[]{:S(2)}, u32[]{:S(2)}) async-start(bf16[16,128,512]{2,1,0:T(8,128)(2,1)} %bitcast.143), calls=%async_computation.1 | async-start | bytes 4194304 | tf_op jit(solution)/shard_map/all_to_all | solution.py:105
  99.0 2.7 %fusion.104 = (bf16[256,1024]{1,0:T(8,128)(2,1)}, bf16[256,1024]{1,0:T(8,128)(2,1)}, bf16[256,1024]{1,0:T(8,128)(2,1)S(1)}, bf16[256,1024]{1,0:T(8,128)(2,1)}) fusion(bf16[256,4096]{1,0:T(8,128)(2,1)} %param.16), kind=kLoop, calls=%fused_computation.138 | loop fusion | bytes 4194304 | tf_op jit(solution)/shard_map/slice | solution.py:88
  105.8 2.1 reshape_reshape.22
  109.3 2.3 fusion.92
  111.6 34.7 %all-to-all-done.1 = bf16[16,128,512]{2,1,0:T(8,128)(2,1)} async-done(((bf16[16,128,512]{2,1,0:T(8,128)(2,1)}), bf16[16,128,512]{2,1,0:T(8,128)(2,1)}, u32[]{:S(2)}, u32[]{:S(2)}) %all-to-all-start.1) | async-done | bytes 2097184 | tf_op jit(solution)/shard_map/all_to_all | solution.py:105
  146.3 3.1 %fusion.89 = (bf16[2304,128]{1,0:T(8,128)(2,1)}, bf16[2304,128]{1,0:T(8,128)(2,1)}, bf16[2304,128]{1,0:T(8,128)(2,1)}, bf16[2304,128]{1,0:T(8,128)(2,1)}) fusion(bf16[2048,512]{1,0:T(8,128)(2,1)} %bitcast.9, bf16[256,512]{1,0:T(8,128)(2,1)} %param.18), kind=kLoop, calls=%fused_computation.104 | loop fusion | flops 4718592 | bytes 4718592 | tf_op jit(solution)/shard_map/concatenate | solution.py:116
  149.5 20.4 %while.52 = (s32[]{:T(128)}, f32[4,512]{1,0:T(4,128)S(1)}, f32[4,512,128]{2,1,0:T(8,128)S(1)}, s32[4,512]{1,0:T(4,128)S(1)}, bf16[4,512,128]{2,1,0:T(8,128)(2,1)...) while((s32[]{:T(128)}, f32[4,512]{1,0:T(4,128)S(1)}, ...), condition=%wide.region_8.9_spmd.clone, body=%wide.region_5.8_spmd.clone.sunk | while | flops 618269696 | bytes 18650016 | solution.py:39
  150.5 2.2 fusion.141
  155.6 2.2 fusion.141
  160.7 2.2 fusion.141
  165.8 2.2 fusion.141
  171.0 22.3 %while.53 = (s32[]{:T(128)}, f32[4,512]{1,0:T(4,128)S(1)}, f32[4,512,128]{2,1,0:T(8,128)}, s32[4,512]{1,0:T(4,128)S(1)}, bf16[4,512,128]{2,1,0:T(8,128)(2,1)}, /...) while((s32[]{:T(128)}, f32[4,512]{1,0:T(4,128)S(1)}, ...), condition=%wide.region_12.13_spmd.clone, body=%wide.region_9.12_spmd.clone.sunk | while | flops 618269696 | bytes 18649756 | solution.py:39
  196.7 23.2 %while.54 = (s32[]{:T(128)}, f32[4,512]{1,0:T(4,128)S(1)}, f32[4,512,128]{2,1,0:T(8,128)}, s32[4,512]{1,0:T(4,128)S(1)}, bf16[4,512,128]{2,1,0:T(8,128)(2,1)}, /...) while((s32[]{:T(128)}, f32[4,512]{1,0:T(4,128)S(1)}, ...), condition=%wide.region_16.17_spmd.clone, body=%wide.region_13.16_spmd.clone.sunk | while | flops 618269696 | bytes 18649756 | solution.py:39
  197.7 2.2 fusion.153
  203.6 2.2 fusion.153
  209.4 2.2 fusion.153
  215.2 2.2 fusion.153
  221.8 22.3 %while.55 = (s32[]{:T(128)}, f32[4,512]{1,0:T(4,128)S(1)}, f32[4,512,128]{2,1,0:T(8,128)}, s32[4,512]{1,0:T(4,128)S(1)}, bf16[4,512,128]{2,1,0:T(8,128)(2,1)}, /...) while((s32[]{:T(128)}, f32[4,512]{1,0:T(4,128)S(1)}, ...), condition=%wide.region_20.21_spmd.clone, body=%wide.region_17.20_spmd.clone.sunk | while | flops 618269696 | bytes 18649756 | solution.py:39
  244.2 2.4 reshape.124
  246.6 2.4 reshape.125
  (224 shorter events, 92.4 us)
Async XLA Ops:
  0.0 37.9 %copy-start = (bf16[32,16,512]{2,1,0:T(8,128)(2,1)S(1)}, bf16[32,16,512]{2,1,0:T(8,128)(2,1)}, u32[]{:S(2)}) copy-start(bf16[32,16,512]{2,1,0:T(8,128)(2,1)} %param.19) | copy-start | bytes 1572868
  39.9 6.6 %copy-start.1 = (bf16[32,16,512]{2,1,0:T(8,128)(2,1)S(1)}, bf16[32,16,512]{2,1,0:T(8,128)(2,1)}, u32[]{:S(2)}) copy-start(bf16[32,16,512]{2,1,0:T(8,128)(2,1)} %param.20) | copy-start | bytes 1572868
  39.9 54.0 %all-to-all-start = ((bf16[16,128,512]{2,1,0:T(8,128)(2,1)}), bf16[16,128,512]{2,1,0:T(8,128)(2,1)S(1)}, u32[]{:S(2)}, u32[]{:S(2)}) async-start(bf16[16,128,512]{2,1,0:T(8,128)(2,1)} %bitcast.144), calls=%async_computation | async-start | bytes 4194304 | tf_op jit(solution)/shard_map/all_to_all | solution.py:98
  48.4 50.3 %copy-start.11 = (s32[1,128]{1,0:T(1,128)S(1)}, s32[1,128]{1,0:T(1,128)}, u32[]{:S(2)}) copy-start(s32[1,128]{1,0:T(1,128)} %param.21) | copy-start | bytes 1540
  93.9 52.4 %all-to-all-start.1 = ((bf16[16,128,512]{2,1,0:T(8,128)(2,1)}), bf16[16,128,512]{2,1,0:T(8,128)(2,1)}, u32[]{:S(2)}, u32[]{:S(2)}) async-start(bf16[16,128,512]{2,1,0:T(8,128)(2,1)} %bitcast.143), calls=%async_computation.1 | async-start | bytes 4194304 | tf_op jit(solution)/shard_map/all_to_all | solution.py:105
  149.4 21.5 %copy-start.6 = (bf16[2304,128]{1,0:T(8,128)(2,1)S(1)}, bf16[2304,128]{1,0:T(8,128)(2,1)}, u32[]{:S(2)}) copy-start(bf16[2304,128]{1,0:T(8,128)(2,1)} %get-tuple-element.706) | copy-start | bytes 1769476
  150.5 2.2 copy-start.8
  155.6 2.2 copy-start.8
  160.7 2.2 copy-start.8
  165.8 2.2 copy-start.8
  172.0 1.9 copy-start.7
  177.6 2.0 copy-start.7
  183.2 2.0 copy-start.7
  188.7 2.0 copy-start.7
  197.7 2.2 copy-start.5
  203.5 2.2 copy-start.5
  209.4 2.2 copy-start.5
  215.2 2.2 copy-start.5
  222.8 2.0 copy-start.4
  228.3 2.0 copy-start.4
  233.9 2.0 copy-start.4
  239.5 2.0 copy-start.4
  244.2 5.2 %copy-start.9 = (f32[256,8]{1,0:T(8,128)S(1)}, f32[256,8]{1,0:T(8,128)}, u32[]{:S(2)}) copy-start(f32[256,8]{1,0:T(8,128)} %div.90) | copy-start | bytes 24580
  250.6 1.5 copy-start.3
  (2 other events, 2.1 us)
where the time goes:
time: 256 us; the launch traced here: 254 us
  waiting for transfers between devices  80.1 us (31%)
  matrix products  55.2 us (22%)
  other arithmetic  39.3 us (15%)
  blocking collectives  37.1 us (14%)
  local copies, waits for them, and re-layouts  30.2 us (12%)
  starting transfers between devices  11.4 us (4%)
    all_to_all x1, waiting for transfers between devices, shards(): lax.all_to_all(sent_keys.reshape(host_count, capacity * page_rows, kv_wid...  45.5 us
    all_to_all x1, waiting for transfers between devices, shards(): lax.all_to_all(sent_values.reshape(host_count, capacity * page_rows, kv_w...  34.7 us
    dot_general x16, matrix products, partial_terms(): lax.dot_general(query_rows, key_rows, (((1,), (1,)), ((), ())), preferred...  32.8 us
    dot_general x16, matrix products, partial_terms(): jnp.dot(weights.astype(jnp.bfloat16), value_rows, preferred_element_type=...  22.4 us
    all_gather x1, blocking collectives, shards(): lax.all_gather(fetch_page, 'hst', axis=0, tiled=True)  21.4 us
    all_gather x1, blocking collectives, shards(): lax.all_gather(fetch_owner, 'hst', axis=0, tiled=True)  15.7 us
    reduce_sum x16, other arithmetic, partial_terms(): weight_sum = jnp.sum(weights, axis=1)  15.6 us
    lt x16, other arithmetic, shards(): (position[:, None] * page_rows + page_offsets[None, :]).reshape(-1) < length  11.7 us
  transfers between devices with their start and end apart: 2, of which 2 were waited for; matrix products, arithmetic and copies ran while one was open for 6% of the time, Pallas kernels for 0%

commit v1 on v0

--- a/solution.py
+++ b/solution.py
@@ -1,6 +1,10 @@
+import functools
+
 import jax
 import jax.numpy as jnp
 from jax import lax
+from jax.experimental import pallas as pl
+from jax.experimental.pallas import tpu as pltpu
 from jax.sharding import PartitionSpec as P
 
 HD = 128
@@ -139,6 +143,387 @@
     return jnp.concatenate(results, axis=1).astype(jnp.bfloat16)
 
 
+PLANE = 4
+LOG2E = 1.4426950408889634
+VMEM_BYTES = 56 * 2**20
+MESH = pl.DeviceIdType.MESH
+
+
+def arrival(source, here, line):
+    far = jnp.abs(source - here)
+    nearer = jnp.minimum(far - 1, here) + jnp.minimum(far - 1, line - 1 - here)
+    after_twin = jnp.logical_and(source > here, here - far >= 0).astype(jnp.int32)
+    return nearer + after_twin + 1
+
+
+def source_of(turn, here, line):
+    found = jnp.int32(0)
+    for candidate in range(line):
+        match = jnp.logical_and(candidate != here, arrival(jnp.int32(candidate), here, line) == turn)
+        found = found + jnp.where(match, candidate, 0)
+    return found
+
+
+def fused_kernel(
+    line,
+    capacity,
+    page_rows,
+    q_ref,
+    sk_ref,
+    sv_ref,
+    ck_ref,
+    cv_ref,
+    table_ref,
+    bias_ref,
+    o_ref,
+    tables,
+    pages_smem,
+    line_buf,
+    picked_from,
+    stage,
+    got,
+    m_ref,
+    acc_ref,
+    table_send,
+    table_recv,
+    local_sem,
+    own_send,
+    line_send,
+    line_recv,
+    plane_send,
+    plane_recv,
+):
+    me = lax.axis_index("hst")
+    here = me // PLANE
+    place = lax.rem(me, PLANE)
+    suffix = q_ref.shape[0]
+    heads = q_ref.shape[1] // HD
+    kv_width = sk_ref.shape[1]
+    group_heads = heads // (kv_width // HD)
+    chunk = capacity * page_rows
+    factor = HD ** (-0.5) * LOG2E
+    caches = (ck_ref, cv_ref)
+
+    def partner(step):
+        return lax.rem(place + step, PLANE)
+
+    def plane_id(where):
+        return {"hst": here * PLANE + where}
+
+    def line_id(where):
+        return {"hst": where * PLANE + place}
+
+    has_side = (here > 0, here < line - 1)
+    toward = (here - 1, here + 1)
+
+    barrier = pltpu.get_barrier_semaphore()
+    for step in range(1, PLANE):
+        pl.semaphore_signal(barrier, inc=1, device_id=plane_id(partner(step)), device_id_type=MESH)
+    for side in range(2):
+
+        @pl.when(has_side[side])
+        def _():
+            pl.semaphore_signal(barrier, inc=1, device_id=line_id(toward[side]), device_id_type=MESH)
+
+    sides = has_side[0].astype(jnp.int32) + has_side[1].astype(jnp.int32)
+    pl.semaphore_wait(barrier, PLANE - 1 + sides)
+
+    def own_copy(side, kind):
+        return pltpu.make_async_remote_copy(
+            src_ref=caches[kind],
+            dst_ref=line_buf.at[1 - side, 0, kind],
+            send_sem=own_send.at[side, kind],
+            recv_sem=line_recv.at[1 - side, 0, kind],
+            device_id=line_id(toward[side]),
+            device_id_type=MESH,
+        )
+
+    def forward_copy(side, far, kind):
+        return pltpu.make_async_remote_copy(
+            src_ref=line_buf.at[side, far - 1, kind],
+            dst_ref=line_buf.at[side, far, kind],
+            send_sem=line_send.at[side, far - 1, kind],
+            recv_sem=line_recv.at[side, far, kind],
+            device_id=line_id(toward[1 - side]),
+            device_id_type=MESH,
+        )
+
+    def table_copy(step):
+        return pltpu.make_async_remote_copy(
+            src_ref=table_ref,
+            dst_ref=tables.at[place],
+            send_sem=table_send.at[step - 1],
+            recv_sem=table_recv.at[place],
+            device_id=plane_id(partner(step)),
+            device_id_type=MESH,
+        )
+
+    def plane_copy(turn, kind, step):
+        return pltpu.make_async_remote_copy(
+            src_ref=stage.at[turn, kind, step - 1],
+            dst_ref=got.at[turn, kind, place],
+            send_sem=plane_send.at[turn, kind, step - 1],
+            recv_sem=plane_recv.at[turn, kind, place],
+            device_id=plane_id(partner(step)),
+            device_id_type=MESH,
+        )
+
+    for step in range(1, PLANE):
+        table_copy(step).start()
+    for kind in range(2):
+        for side in range(2):
+
+            @pl.when(has_side[side])
+            def _():
+                own_copy(side, kind).start()
+
+    own_table = pltpu.make_async_copy(table_ref, tables.at[place], local_sem.at[0])
+    own_table.start()
+    own_table.wait()
+    for step in range(1, PLANE):
+        from_there = pltpu.make_async_remote_copy(
+            src_ref=table_ref,
+            dst_ref=tables.at[partner(step)],
+            send_sem=table_send.at[step - 1],
+            recv_sem=table_recv.at[partner(step)],
+            device_id=plane_id(partner(step)),
+            device_id_type=MESH,
+        )
+        from_there.wait()
+    to_smem = pltpu.make_async_copy(tables, pages_smem, local_sem.at[1])
+    to_smem.start()
+    to_smem.wait()
+
+    def pick_and_send(source, turn, kind, from_ref):
+        first = (source * PLANE + place) * capacity
+        for step in range(1, PLANE):
+            who = partner(step)
+
+            def one_page(j, carry):
+                page = pages_smem[who, 0, first + j]
+                stage[turn, kind, step - 1, pl.ds(pl.multiple_of(j * page_rows, page_rows), page_rows)] = (
+                    from_ref[page]
+                )
+                return carry
+
+            lax.fori_loop(0, capacity, one_page, 0, unroll=True)
+            plane_copy(turn, kind, step).start()
+
+        def own_page(j, carry):
+            page = pages_smem[place, 0, first + j]
+            got[turn, kind, place, pl.ds(pl.multiple_of(j * page_rows, page_rows), page_rows)] = from_ref[
+                page
+            ]
+            return carry
+
+        lax.fori_loop(0, capacity, own_page, 0, unroll=True)
+
+    def event(far, kind):
+        for side in range(2):
+            source = here - far if side == 0 else here + far
+            valid = source >= 0 if side == 0 else source < line
+
+            @pl.when(valid)
+            def _():
+                pltpu.make_async_remote_copy(
+                    src_ref=line_buf.at[side, far - 1, kind],
+                    dst_ref=line_buf.at[side, far - 1, kind],
+                    send_sem=line_send.at[side, far - 1, kind],
+                    recv_sem=line_recv.at[side, far - 1, kind],
+                    device_id=line_id(source),
+                    device_id_type=MESH,
+                ).wait_recv()
+                if far < line - 1:
+
+                    @pl.when(has_side[1 - side])
+                    def _():
+                        forward_copy(side, far, kind).start()
+
+                picked_from[...] = line_buf[side, far - 1, kind]
+                pick_and_send(source, arrival(source, here, line), kind, picked_from)
+
+    def wait_plane(turn, kind):
+        for step in range(1, PLANE):
+            there = partner(step)
+            pltpu.make_async_remote_copy(
+                src_ref=stage.at[turn, kind, step - 1],
+                dst_ref=got.at[turn, kind, there],
+                send_sem=plane_send.at[turn, kind, step - 1],
+                recv_sem=plane_recv.at[turn, kind, there],
+                device_id=plane_id(there),
+                device_id_type=MESH,
+            ).wait()
+
+    def attend(first_head, last_head, key_of, value_of, bias_of, count, first, last):
+        width = 2
+
+        def heads_step(pair, carry):
+            base = first_head + pair * width
+            kv_head = base // group_heads
+            columns = pl.ds(pl.multiple_of(kv_head * HD, HD), HD)
+            key_rows = key_of(columns)
+            value_rows = value_of(columns)
+            values = jnp.concatenate([value_rows, jnp.ones_like(value_rows)], axis=1)
+            for inner in range(width):
+                head = base + inner
+                head_columns = pl.ds(pl.multiple_of(head * HD, HD), HD)
+                scores = lax.dot_general(
+                    q_ref[:, head_columns],
+                    key_rows,
+                    (((1,), (1,)), ((), ())),
+                    preferred_element_type=jnp.float32,
+                )
+                scores = bias_of(scores * factor)
+                top = jnp.max(scores, axis=1, keepdims=True)
+                if first:
+                    new_max = jnp.broadcast_to(top, (suffix, HD))
+                else:
+                    old_max = m_ref[head]
+                    new_max = jnp.maximum(old_max, top)
+                weights = jnp.concatenate(
+                    [
+                        jnp.exp2(scores[:, tile * HD : (tile + 1) * HD] - new_max).astype(jnp.bfloat16)
+                        for tile in range(count // HD)
+                    ],
+                    axis=1,
+                )
+                summed = jnp.dot(weights, values, preferred_element_type=jnp.float32)
+                if not first:
+                    shrink = jnp.exp2(old_max - new_max)
+                    summed = acc_ref[head] * jnp.concatenate([shrink, shrink], axis=1) + summed
+                if last:
+                    o_ref[:, head_columns] = (summed[:, :HD] / summed[:, HD:]).astype(jnp.bfloat16)
+                else:
+                    acc_ref[head] = summed
+                    m_ref[head] = new_max
+            return carry
+
+        lax.fori_loop(0, (last_head - first_head) // width, heads_step, 0)
+
+    def attend_suffix():
+        causal = lax.broadcasted_iota(jnp.int32, (suffix, suffix), 1) <= lax.broadcasted_iota(
+            jnp.int32, (suffix, suffix), 0
+        )
+        attend(
+            0,
+            heads,
+            lambda columns: sk_ref[:, columns],
+            lambda columns: sv_ref[:, columns],
+            lambda scores: jnp.where(causal, scores, MASKED),
+            suffix,
+            True,
+            False,
+        )
+
+    def attend_group(turn, source, first_head, last_head, last):
+        bias = bias_ref[source]
+
+        def rows_of(kind):
+            return lambda columns: got[turn, kind, :, :, columns].reshape(PLANE * chunk, HD)
+
+        attend(
+            first_head,
+            last_head,
+            rows_of(0),
+            rows_of(1),
+            lambda scores: scores + bias,
+            PLANE * chunk,
+            False,
+            last,
+        )
+
+    pick_and_send(here, 0, 0, ck_ref)
+    pick_and_send(here, 0, 1, cv_ref)
+    attend_suffix()
+    wait_plane(0, 0)
+    wait_plane(0, 1)
+    for turn in range(1, line):
+        before = here if turn == 1 else source_of(turn - 1, here, line)
+        event(turn, 0)
+        attend_group(turn - 1, before, 0, heads // 2, False)
+        event(turn, 1)
+        attend_group(turn - 1, before, heads // 2, heads, False)
+        wait_plane(turn, 0)
+        wait_plane(turn, 1)
+    attend_group(line - 1, source_of(line - 1, here, line), 0, heads, True)
+
+    for kind in range(2):
+        for side in range(2):
+
+            @pl.when(has_side[side])
+            def _():
+                own_copy(side, kind).wait_send()
+
+            for far in range(1, line - 1):
+                source = here - far if side == 0 else here + far
+                valid = source >= 0 if side == 0 else source < line
+
+                @pl.when(jnp.logical_and(valid, has_side[1 - side]))
+                def _():
+                    forward_copy(side, far, kind).wait_send()
+
+
+def fused(queries, suf_keys, suf_values, cache_keys, cache_values, fetch_owner, fetch_page, prefix_len):
+    host_count = lax.axis_size("hst")
+    line = host_count // PLANE
+    slot_count = fetch_owner.shape[1]
+    capacity = slot_count // host_count
+    own_pages, page_rows, kv_width = cache_keys.shape
+    suffix = queries.shape[0]
+    heads = queries.shape[1] // HD
+    owners = fetch_owner[0]
+    slot_ids = jnp.arange(slot_count, dtype=jnp.int32)
+    earlier = jnp.logical_and(
+        owners[None, :] == owners[:, None], slot_ids[None, :] < slot_ids[:, None]
+    )
+    rank = jnp.sum(earlier.astype(jnp.int32), axis=1)
+    slot_of = owners * capacity + rank
+    match = slot_of[None, :] == slot_ids[:, None]
+    pages = jnp.sum(jnp.where(match, fetch_page, 0), axis=1)
+    position = jnp.sum(jnp.where(match, slot_ids[None, :], 0), axis=1)
+    table = jnp.broadcast_to(pages[None, :], (8, slot_count))
+    row_ids = jnp.arange(page_rows, dtype=jnp.int32)
+    seen = position[:, None] * page_rows + row_ids[None, :] < prefix_len[0]
+    bias = jnp.where(seen, jnp.float32(0.0), jnp.float32(MASKED)).reshape(line, 1, PLANE * capacity * page_rows)
+    vmem = pl.BlockSpec(memory_space=pltpu.VMEM)
+    chunk = capacity * page_rows
+    shard = (own_pages, page_rows, kv_width)
+    dma = pltpu.SemaphoreType.DMA
+    return pl.pallas_call(
+        functools.partial(fused_kernel, line, capacity, page_rows),
+        out_shape=jax.ShapeDtypeStruct(queries.shape, jnp.bfloat16),
+        in_specs=[vmem] * 7,
+        out_specs=vmem,
+        scratch_shapes=[
+            pltpu.VMEM((PLANE, 8, slot_count), jnp.int32),
+            pltpu.SMEM((PLANE, 8, slot_count), jnp.int32),
+            pltpu.VMEM((2, line - 1, 2) + shard, jnp.bfloat16),
+            pltpu.VMEM(shard, jnp.bfloat16),
+            pltpu.VMEM((line, 2, PLANE - 1, chunk, kv_width), jnp.bfloat16),
+            pltpu.VMEM((line, 2, PLANE, chunk, kv_width), jnp.bfloat16),
+            pltpu.VMEM((heads, suffix, HD), jnp.float32),
+            pltpu.VMEM((heads, suffix, 2 * HD), jnp.float32),
+            dma((PLANE - 1,)),
+            dma((PLANE,)),
+            dma((2,)),
+            dma((2, 2)),
+            dma((2, line - 1, 2)),
+            dma((2, line - 1, 2)),
+            dma((line, 2, PLANE - 1)),
+            dma((line, 2, PLANE)),
+        ],
+        compiler_params=pltpu.CompilerParams(
+            collective_id=0, has_side_effects=True, vmem_limit_bytes=VMEM_BYTES
+        ),
+    )(queries, suf_keys, suf_values, cache_keys, cache_values, table, bias)
+
+
+def fits(mesh, cache_shape):
+    hosts = mesh.shape["hst"]
+    own_bytes = 2 * 2 * cache_shape[1] * cache_shape[2] * cache_shape[0] // mesh.size
+    return hosts % PLANE == 0 and hosts > PLANE and 2 * (hosts // PLANE - 1) * own_bytes <= 8 * 2**20
+
+
 def solution(mesh):
     in_specs = (
         P(("dom", "hst"), None),
@@ -151,4 +536,11 @@
         P(("dom", "hst")),
     )
     out_specs = P(("dom", "hst"), None)
-    return jax.shard_map(shards, mesh=mesh, in_specs=in_specs, out_specs=out_specs, check_vma=False)
+
+    def run(*args):
+        body = fused if fits(mesh, args[3].shape) else shards
+        return jax.shard_map(
+            body, mesh=mesh, in_specs=in_specs, out_specs=out_specs, check_vma=False
+        )(*args)
+
+    return run

time: 256 us -> 103 us (0.40)
  the two profiles are of different devices: /device:TPU:13 before, /device:TPU:1 now
where the time goes in v1:
time: 103 us; the launch traced here: 102 us
  Pallas kernels  94.7 us (92%)
  local copies, waits for them, and re-layouts  4.08 us (4%)
  other arithmetic  2.94 us (3%)
    pallas_call x1, Pallas kernels, fused(): pl.pallas_call(functools.partial(fused_kernel, line, capacity, page_rows)...  94.7 us
    unnamed x1, local copies, waits for them, and re-layouts  3.13 us

profile of v1, /device:TPU:1, one launch (start us, length us, event | category | flops | bytes accessed | tf_op | source)
XLA Modules:
  0.0 102.5 jit_solution(11761674216760443740)
XLA Ops:
  0.7 0.9 convert_reduce_fusion
  1.6 0.7 fusion.1
  2.2 0.8 select_reduce_fusion
  3.0 0.1 mul.25
  3.1 0.6 broadcast_in_dim.42.table_ref
  3.7 0.1 add.34
  3.8 0.1 add.31
  3.8 0.1 add.37
  4.0 0.6 compare_select_fusion.bias_ref
  4.6 94.7 %shard_map.82 = bf16[256,4096]{1,0:T(8,128)(2,1)} custom-call(bf16[256,4096]{1,0:T(8,128)(2,1)} %q_ref.1, bf16[256,512]{1,0:T(8,128)(2,1)} %sk_ref.1, bf16[256,512]{1,0:T(8,128)(2,1)} %sv_ref.1, bf16[32,16,512]{2,1,0:T(8,128)(2,1)} %ck_ref.1, bf16[32,16,512]{2,1,0:T(8,128)(2,1)} %cv_ref.1, s32[8,128]{1,0:T(8,128)} %broadcast_in_dim.42.table_ref, ...), custom_call_target="tpu_custom_call" | custom-call | tf_op jit(solution)/shard_map/pallas_call | solution.py:492
  99.3 3.1 %copy.13 = bf16[256,4096]{1,0:T(8,128)(2,1)} copy(bf16[256,4096]{1,0:T(8,128)(2,1)} %shard_map.82) | data formatting | bytes 4194304
  (2 shorter events, 0.0 us)

commit v2 on v1

--- a/solution.py
+++ b/solution.py
@@ -144,6 +144,8 @@
 
 
 PLANE = 4
+WIDTH = 8
+TURN_KEYS = False
 LOG2E = 1.4426950408889634
 VMEM_BYTES = 56 * 2**20
 MESH = pl.DeviceIdType.MESH
@@ -173,15 +175,22 @@
     sv_ref,
     ck_ref,
     cv_ref,
+    owner_ref,
+    page_ref,
+    len_ref,
+    o_ref,
     table_ref,
-    bias_ref,
-    o_ref,
     tables,
     pages_smem,
+    keep_ref,
     line_buf,
     picked_from,
     stage,
     got,
+    scaled_q,
+    key_block,
+    value_block,
+    weights_ref,
     m_ref,
     acc_ref,
     table_send,
@@ -228,6 +237,36 @@
     sides = has_side[0].astype(jnp.int32) + has_side[1].astype(jnp.int32)
     pl.semaphore_wait(barrier, PLANE - 1 + sides)
 
+    def make_table():
+        slots = owner_ref.shape[1]
+        square = (slots, slots)
+        down = lax.broadcasted_iota(jnp.int32, square, 0)
+        across = lax.broadcasted_iota(jnp.int32, square, 1)
+        owner_row = jnp.broadcast_to(owner_ref[...], square)
+        owner_column = jnp.transpose(owner_row)
+        page_column = jnp.transpose(jnp.broadcast_to(page_ref[...], square))
+        same = owner_row == owner_column
+        rank_row = jnp.sum(
+            jnp.where(jnp.logical_and(same, down < across), 1, 0), axis=0, keepdims=True
+        )
+        slot_row = jnp.broadcast_to(owner_row[:1] * capacity + rank_row, square)
+        slot_column = jnp.transpose(slot_row)
+        pages = jnp.sum(
+            jnp.where(slot_column == across, page_column, 0), axis=0, keepdims=True
+        )
+        pages = jnp.clip(pages, 0, ck_ref.shape[0] - 1)
+        table_ref[...] = jnp.broadcast_to(pages, table_ref.shape)
+        position = jnp.sum(
+            jnp.where(slot_row == down, across, 0).astype(jnp.float32),
+            axis=1,
+            keepdims=True,
+        )
+        by_row = jnp.broadcast_to(position.reshape(slots, 1, 1), (slots, page_rows, HD))
+        in_page = lax.broadcasted_iota(jnp.int32, by_row.shape, 1).astype(jnp.float32)
+        limit = len_ref[0].astype(jnp.float32)
+        keep = jnp.where(by_row * page_rows + in_page < limit, 1.0, 0.0).astype(jnp.bfloat16)
+        keep_ref[...] = keep.reshape(keep_ref.shape)
+
     def own_copy(side, kind):
         return pltpu.make_async_remote_copy(
             src_ref=caches[kind],
@@ -268,14 +307,16 @@
             device_id_type=MESH,
         )
 
-    for step in range(1, PLANE):
-        table_copy(step).start()
     for kind in range(2):
         for side in range(2):
 
             @pl.when(has_side[side])
             def _():
                 own_copy(side, kind).start()
+
+    make_table()
+    for step in range(1, PLANE):
+        table_copy(step).start()
 
     own_table = pltpu.make_async_copy(table_ref, tables.at[place], local_sem.at[0])
     own_table.start()
@@ -354,98 +395,148 @@
                 device_id_type=MESH,
             ).wait()
 
-    def attend(first_head, last_head, key_of, value_of, bias_of, count, first, last):
-        width = 2
-
-        def heads_step(pair, carry):
-            base = first_head + pair * width
-            kv_head = base // group_heads
+    kv_heads = kv_width // HD
+    count = PLANE * chunk
+
+    def load_keys(kv_head, key_rows, keep):
+        if keep is not None:
             columns = pl.ds(pl.multiple_of(kv_head * HD, HD), HD)
-            key_rows = key_of(columns)
-            value_rows = value_of(columns)
-            values = jnp.concatenate([value_rows, jnp.ones_like(value_rows)], axis=1)
-            for inner in range(width):
-                head = base + inner
-                head_columns = pl.ds(pl.multiple_of(head * HD, HD), HD)
-                scores = lax.dot_general(
-                    q_ref[:, head_columns],
-                    key_rows,
-                    (((1,), (1,)), ((), ())),
-                    preferred_element_type=jnp.float32,
-                )
-                scores = bias_of(scores * factor)
-                top = jnp.max(scores, axis=1, keepdims=True)
-                if first:
-                    new_max = jnp.broadcast_to(top, (suffix, HD))
-                else:
-                    old_max = m_ref[head]
-                    new_max = jnp.maximum(old_max, top)
-                weights = jnp.concatenate(
-                    [
-                        jnp.exp2(scores[:, tile * HD : (tile + 1) * HD] - new_max).astype(jnp.bfloat16)
-                        for tile in range(count // HD)
-                    ],
-                    axis=1,
-                )
-                summed = jnp.dot(weights, values, preferred_element_type=jnp.float32)
-                if not first:
-                    shrink = jnp.exp2(old_max - new_max)
-                    summed = acc_ref[head] * jnp.concatenate([shrink, shrink], axis=1) + summed
-                if last:
-                    o_ref[:, head_columns] = (summed[:, :HD] / summed[:, HD:]).astype(jnp.bfloat16)
-                else:
-                    acc_ref[head] = summed
-                    m_ref[head] = new_max
+            key_rows = key_rows * keep + sk_ref[0:1, columns] * (1 - keep)
+        if TURN_KEYS:
+            turned = jnp.transpose(key_rows)
+            key_block[0:HD, : key_rows.shape[0]] = turned
+            key_block[HD : 2 * HD, : key_rows.shape[0]] = turned
+        else:
+            key_block[: key_rows.shape[0], :HD] = key_rows
+            key_block[: key_rows.shape[0], HD:] = key_rows
+
+    def load_values(value_rows, keep):
+        rows = value_rows.shape[0]
+        value_block[:rows, :HD] = value_rows if keep is None else value_rows * keep
+        value_block[:rows, HD:] = jnp.ones_like(value_rows) if keep is None else keep
+
+    def scores_of(query_rows, keys):
+        if TURN_KEYS:
+            return jnp.dot(query_rows, key_block[:, :keys], preferred_element_type=jnp.float32)
+        return lax.dot_general(
+            query_rows, key_block[:keys], (((1,), (1,)), ((), ())), preferred_element_type=jnp.float32
+        )
+
+    def each_kv_head(load, one_head):
+        def kv_step(kv_head, carry):
+            load(kv_head)
+
+            def heads_step(part, inner_carry):
+                for inner in range(WIDTH):
+                    one_head(kv_head * group_heads + part * WIDTH + inner)
+                return inner_carry
+
+            lax.fori_loop(0, group_heads // WIDTH, heads_step, 0)
             return carry
 
-        lax.fori_loop(0, (last_head - first_head) // width, heads_step, 0)
+        lax.fori_loop(0, kv_heads, kv_step, 0)
+
+    def weigh(scores, top):
+        return jnp.concatenate(
+            [
+                jnp.exp2(scores[:, tile * HD : (tile + 1) * HD] - top).astype(jnp.bfloat16)
+                for tile in range(scores.shape[1] // HD)
+            ],
+            axis=1,
+        )
 
     def attend_suffix():
         causal = lax.broadcasted_iota(jnp.int32, (suffix, suffix), 1) <= lax.broadcasted_iota(
             jnp.int32, (suffix, suffix), 0
         )
-        attend(
-            0,
-            heads,
-            lambda columns: sk_ref[:, columns],
-            lambda columns: sv_ref[:, columns],
-            lambda scores: jnp.where(causal, scores, MASKED),
-            suffix,
-            True,
-            False,
-        )
-
-    def attend_group(turn, source, first_head, last_head, last):
-        bias = bias_ref[source]
-
-        def rows_of(kind):
-            return lambda columns: got[turn, kind, :, :, columns].reshape(PLANE * chunk, HD)
-
-        attend(
-            first_head,
-            last_head,
-            rows_of(0),
-            rows_of(1),
-            lambda scores: scores + bias,
-            PLANE * chunk,
-            False,
-            last,
-        )
+
+        def load(kv_head):
+            columns = pl.ds(pl.multiple_of(kv_head * HD, HD), HD)
+            load_keys(kv_head, sk_ref[:, columns], None)
+            load_values(sv_ref[:, columns], None)
+
+        def one_head(head):
+            scaled = q_ref[:, pl.ds(pl.multiple_of(head * HD, HD), HD)].astype(jnp.float32) * factor
+            high = scaled.astype(jnp.bfloat16)
+            low = (scaled - high.astype(jnp.float32)).astype(jnp.bfloat16)
+            both = jnp.concatenate([high, low], axis=1)
+            scaled_q[head] = both
+            scores = jnp.where(causal, scores_of(both, suffix), MASKED)
+            top = jnp.broadcast_to(jnp.max(scores, axis=1, keepdims=True), (suffix, HD))
+            weights = weigh(scores, top)
+            m_ref[head] = top
+            acc_ref[head] = jnp.dot(weights, value_block[:suffix], preferred_element_type=jnp.float32)
+
+        each_kv_head(load, one_head)
+
+    def group_rows(turn, kind, kv_head):
+        columns = pl.ds(pl.multiple_of(kv_head * HD, HD), HD)
+        return got[turn, kind, :, :, columns].reshape(count, HD)
+
+    def new_weights(head):
+        scores = scores_of(scaled_q[head], count)
+        old = m_ref[head]
+        top = jnp.maximum(old, jnp.max(scores, axis=1, keepdims=True))
+        shrink = jnp.exp2(old - top)
+        m_ref[head] = top
+        return weigh(scores, top), jnp.concatenate([shrink, shrink], axis=1) * acc_ref[head]
+
+    def attend_group(turn, source):
+        def load(kv_head):
+            load_keys(kv_head, group_rows(turn, 0, kv_head), keep_ref[source])
+            load_values(group_rows(turn, 1, kv_head), keep_ref[source])
+
+        def one_head(head):
+            weights, kept = new_weights(head)
+            acc_ref[head] = kept + jnp.dot(weights, value_block[...], preferred_element_type=jnp.float32)
+
+        each_kv_head(load, one_head)
+
+    def last_weights(turn, source):
+        def load(kv_head):
+            load_keys(kv_head, group_rows(turn, 0, kv_head), keep_ref[source])
+
+        def one_head(head):
+            weights, kept = new_weights(head)
+            weights_ref[head] = weights
+            acc_ref[head] = kept
+
+        each_kv_head(load, one_head)
+
+    def last_sums(turn, source):
+        def load(kv_head):
+            load_values(group_rows(turn, 1, kv_head), keep_ref[source])
+
+        def one_head(head):
+            summed = acc_ref[head] + jnp.dot(
+                weights_ref[head], value_block[...], preferred_element_type=jnp.float32
+            )
+            o_ref[:, pl.ds(pl.multiple_of(head * HD, HD), HD)] = (summed[:, :HD] / summed[:, HD:]).astype(
+                jnp.bfloat16
+            )
+
+        each_kv_head(load, one_head)
 
     pick_and_send(here, 0, 0, ck_ref)
     pick_and_send(here, 0, 1, cv_ref)
     attend_suffix()
     wait_plane(0, 0)
     wait_plane(0, 1)
-    for turn in range(1, line):
-        before = here if turn == 1 else source_of(turn - 1, here, line)
+    last = line - 1
+    for turn in range(1, last):
         event(turn, 0)
-        attend_group(turn - 1, before, 0, heads // 2, False)
+        attend_group(turn - 1, here if turn == 1 else source_of(turn - 1, here, line))
         event(turn, 1)
-        attend_group(turn - 1, before, heads // 2, heads, False)
         wait_plane(turn, 0)
         wait_plane(turn, 1)
-    attend_group(line - 1, source_of(line - 1, here, line), 0, heads, True)
+    attend_group(last - 1, source_of(last - 1, here, line))
+    last_source = source_of(last, here, line)
+    event(last, 0)
+    wait_plane(last, 0)
+    last_weights(last, last_source)
+    event(last, 1)
+    wait_plane(last, 1)
+    last_sums(last, last_source)
 
     for kind in range(2):
         for side in range(2):
@@ -471,20 +562,6 @@
     own_pages, page_rows, kv_width = cache_keys.shape
     suffix = queries.shape[0]
     heads = queries.shape[1] // HD
-    owners = fetch_owner[0]
-    slot_ids = jnp.arange(slot_count, dtype=jnp.int32)
-    earlier = jnp.logical_and(
-        owners[None, :] == owners[:, None], slot_ids[None, :] < slot_ids[:, None]
-    )
-    rank = jnp.sum(earlier.astype(jnp.int32), axis=1)
-    slot_of = owners * capacity + rank
-    match = slot_of[None, :] == slot_ids[:, None]
-    pages = jnp.sum(jnp.where(match, fetch_page, 0), axis=1)
-    position = jnp.sum(jnp.where(match, slot_ids[None, :], 0), axis=1)
-    table = jnp.broadcast_to(pages[None, :], (8, slot_count))
-    row_ids = jnp.arange(page_rows, dtype=jnp.int32)
-    seen = position[:, None] * page_rows + row_ids[None, :] < prefix_len[0]
-    bias = jnp.where(seen, jnp.float32(0.0), jnp.float32(MASKED)).reshape(line, 1, PLANE * capacity * page_rows)
     vmem = pl.BlockSpec(memory_space=pltpu.VMEM)
     chunk = capacity * page_rows
     shard = (own_pages, page_rows, kv_width)
@@ -492,15 +569,21 @@
     return pl.pallas_call(
         functools.partial(fused_kernel, line, capacity, page_rows),
         out_shape=jax.ShapeDtypeStruct(queries.shape, jnp.bfloat16),
-        in_specs=[vmem] * 7,
+        in_specs=[vmem] * 7 + [pl.BlockSpec(memory_space=pltpu.SMEM)],
         out_specs=vmem,
         scratch_shapes=[
+            pltpu.VMEM((8, slot_count), jnp.int32),
             pltpu.VMEM((PLANE, 8, slot_count), jnp.int32),
             pltpu.SMEM((PLANE, 8, slot_count), jnp.int32),
+            pltpu.VMEM((line, PLANE * chunk, HD), jnp.bfloat16),
             pltpu.VMEM((2, line - 1, 2) + shard, jnp.bfloat16),
             pltpu.VMEM(shard, jnp.bfloat16),
             pltpu.VMEM((line, 2, PLANE - 1, chunk, kv_width), jnp.bfloat16),
             pltpu.VMEM((line, 2, PLANE, chunk, kv_width), jnp.bfloat16),
+            pltpu.VMEM((heads, suffix, 2 * HD), jnp.bfloat16),
+            pltpu.VMEM((2 * HD, PLANE * chunk) if TURN_KEYS else (PLANE * chunk, 2 * HD), jnp.bfloat16),
+            pltpu.VMEM((PLANE * chunk, 2 * HD), jnp.bfloat16),
+            pltpu.VMEM((heads, suffix, PLANE * chunk), jnp.bfloat16),
             pltpu.VMEM((heads, suffix, HD), jnp.float32),
             pltpu.VMEM((heads, suffix, 2 * HD), jnp.float32),
             dma((PLANE - 1,)),
@@ -515,7 +598,7 @@
         compiler_params=pltpu.CompilerParams(
             collective_id=0, has_side_effects=True, vmem_limit_bytes=VMEM_BYTES
         ),
-    )(queries, suf_keys, suf_values, cache_keys, cache_values, table, bias)
+    )(queries, suf_keys, suf_values, cache_keys, cache_values, fetch_owner, fetch_page, prefix_len)
 
 
 def fits(mesh, cache_shape):

time: 103 us -> 93.6 us (0.909)
  Pallas kernels: 94.7 us -> 89.6 us
  other arithmetic: 2.94 us -> 0 us
    pallas_call x1, Pallas kernels: 94.7 us -> 89.6 us  [fused(): pl.pallas_call(functools.partial(fused_kernel, line, capacity, page_rows)...]
    reduce_sum x2 -> x0, other arithmetic: 1.66 us -> none  [the longest x1 0.9 us: fused(): rank = jnp.sum(earlier.astype(jnp.int32), axis=1)]
where the time goes in v2:
time: 93.6 us; the launch traced here: 93.4 us
  Pallas kernels  89.6 us (96%)
  local copies, waits for them, and re-layouts  3.13 us (3%)
    pallas_call x1, Pallas kernels, fused(): pl.pallas_call(functools.partial(fused_kernel, line, capacity, page_rows)...  89.6 us
    unnamed x1, local copies, waits for them, and re-layouts  3.13 us

profile of v2, /device:TPU:1, one launch (start us, length us, event | category | flops | bytes accessed | tf_op | source)
XLA Modules:
  0.0 93.4 jit_solution(12434423013755152653)
XLA Ops:
  0.7 89.6 %shard_map.82 = bf16[256,4096]{1,0:T(8,128)(2,1)} custom-call(bf16[256,4096]{1,0:T(8,128)(2,1)} %q_ref.1, bf16[256,512]{1,0:T(8,128)(2,1)} %sk_ref.1, bf16[256,512]{1,0:T(8,128)(2,1)} %sv_ref.1, bf16[32,16,512]{2,1,0:T(8,128)(2,1)} %ck_ref.1, bf16[32,16,512]{2,1,0:T(8,128)(2,1)} %cv_ref.1, s32[1,128]{1,0:T(1,128)} %owner_ref.1, s32[1,128]{1,0:T(1,128)} %page_ref.1, ...), custom_call_target="tpu_custom_call" | custom-call | tf_op jit(solution)/shard_map/pallas_call | solution.py:569
  90.3 3.1 %copy.11 = bf16[256,4096]{1,0:T(8,128)(2,1)} copy(bf16[256,4096]{1,0:T(8,128)(2,1)} %shard_map.82) | data formatting | bytes 4194304

commit v3 on v2

--- a/solution.py
+++ b/solution.py
@@ -422,7 +422,7 @@
             query_rows, key_block[:keys], (((1,), (1,)), ((), ())), preferred_element_type=jnp.float32
         )
 
-    def each_kv_head(load, one_head):
+    def each_kv_head(load, one_head, part=(0, kv_heads)):
         def kv_step(kv_head, carry):
             load(kv_head)
 
@@ -434,7 +434,7 @@
             lax.fori_loop(0, group_heads // WIDTH, heads_step, 0)
             return carry
 
-        lax.fori_loop(0, kv_heads, kv_step, 0)
+        lax.fori_loop(part[0], part[1], kv_step, 0)
 
     def weigh(scores, top):
         return jnp.concatenate(
@@ -481,7 +481,7 @@
         m_ref[head] = top
         return weigh(scores, top), jnp.concatenate([shrink, shrink], axis=1) * acc_ref[head]
 
-    def attend_group(turn, source):
+    def attend_group(turn, source, part=(0, kv_heads)):
         def load(kv_head):
             load_keys(kv_head, group_rows(turn, 0, kv_head), keep_ref[source])
             load_values(group_rows(turn, 1, kv_head), keep_ref[source])
@@ -490,9 +490,9 @@
             weights, kept = new_weights(head)
             acc_ref[head] = kept + jnp.dot(weights, value_block[...], preferred_element_type=jnp.float32)
 
-        each_kv_head(load, one_head)
-
-    def last_weights(turn, source):
+        each_kv_head(load, one_head, part)
+
+    def last_weights(turn, source, part):
         def load(kv_head):
             load_keys(kv_head, group_rows(turn, 0, kv_head), keep_ref[source])
 
@@ -501,7 +501,7 @@
             weights_ref[head] = weights
             acc_ref[head] = kept
 
-        each_kv_head(load, one_head)
+        each_kv_head(load, one_head, part)
 
     def last_sums(turn, source):
         def load(kv_head):
@@ -529,12 +529,16 @@
         event(turn, 1)
         wait_plane(turn, 0)
         wait_plane(turn, 1)
-    attend_group(last - 1, source_of(last - 1, here, line))
+    halves = ((0, kv_heads // 2), (kv_heads // 2, kv_heads))
     last_source = source_of(last, here, line)
+    before = source_of(last - 1, here, line)
+    attend_group(last - 1, before, halves[0])
     event(last, 0)
+    attend_group(last - 1, before, halves[1])
     wait_plane(last, 0)
-    last_weights(last, last_source)
+    last_weights(last, last_source, halves[0])
     event(last, 1)
+    last_weights(last, last_source, halves[1])
     wait_plane(last, 1)
     last_sums(last, last_source)
 

time: 93.6 us -> 90.1 us (0.963)
  Pallas kernels: 89.6 us -> 86.2 us
    pallas_call x1, Pallas kernels: 89.6 us -> 86.2 us  [fused(): pl.pallas_call(functools.partial(fused_kernel, line, capacity, page_rows)...]
where the time goes in v3:
time: 90.1 us; the launch traced here: 90 us
  Pallas kernels  86.2 us (96%)
  local copies, waits for them, and re-layouts  3.13 us (3%)
    pallas_call x1, Pallas kernels, fused(): pl.pallas_call(functools.partial(fused_kernel, line, capacity, page_rows)...  86.2 us
    unnamed x1, local copies, waits for them, and re-layouts  3.13 us

profile of v3, /device:TPU:1, one launch (start us, length us, event | category | flops | bytes accessed | tf_op | source)
XLA Modules:
  0.0 90.0 jit_solution(10017039922741406370)
XLA Ops:
  0.7 86.2 %shard_map.82 = bf16[256,4096]{1,0:T(8,128)(2,1)} custom-call(bf16[256,4096]{1,0:T(8,128)(2,1)} %q_ref.1, bf16[256,512]{1,0:T(8,128)(2,1)} %sk_ref.1, bf16[256,512]{1,0:T(8,128)(2,1)} %sv_ref.1, bf16[32,16,512]{2,1,0:T(8,128)(2,1)} %ck_ref.1, bf16[32,16,512]{2,1,0:T(8,128)(2,1)} %cv_ref.1, s32[1,128]{1,0:T(1,128)} %owner_ref.1, s32[1,128]{1,0:T(1,128)} %page_ref.1, ...), custom_call_target="tpu_custom_call" | custom-call | tf_op jit(solution)/shard_map/pallas_call | solution.py:573
  86.8 3.1 %copy.11 = bf16[256,4096]{1,0:T(8,128)(2,1)} copy(bf16[256,4096]{1,0:T(8,128)(2,1)} %shard_map.82) | data formatting | bytes 4194304
